TPU v7x, 128 devices: a whole 4x4x4 slice. The times are simulated.
128 devices in a mesh: curve: 64 (over z, y, x), aux: 2 (over core).
Axes of the slice: x: 4, y: 4, z: 4, core: 2. Of those that a mesh axis runs over, the one named last changes fastest.
Arguments:
- coeffs: bfloat16 [128, 12800, 320], P('curve', 'aux'), may hold values from -6 to 6
- kernel: bfloat16 [512, 320, 320], P('curve'), may hold values from -0.3125 to 0.3125
- metric: float32 [128, 12800], P(None, 'aux'), may hold values from 0.5 to 2
- counts: int32 [128], replicated, may hold values from 6500 to 12800, as said below
- pairs: int32 [512, 2], P('curve'), may hold values from 0 to 127, as said below
Outputs:
- exchange: float32 [128, 320, 320], P('curve', 'aux')
Inputs may be any that keep to these rules, and one draw needn't show every extreme that they name: counts are 100 times a block's atom count; some block has all 12800. `pairs`: rows 8 * d to 8 * d + 7 name as first block one of blocks 2 * d to 2 * d + 1 and as second block one of blocks 2 * d - 2 to 2 * d + 2 * 2 - 1; every existing block of that range is named by some row of these.
All inputs are finite; a program needn't handle non-finite values.
Results may differ from a plain program's by a relative error of at most 0.0025.
Values may be sent and summed in bfloat16 or wider, within the bound.
A program may use at most 128 MiB of HBM per device.

v0:
```python
import jax
import jax.numpy as jnp
from jax import lax
from jax.sharding import PartitionSpec as P

NG = 320
AUXB = 12800


def extended(value, sides, width):
    for axis, dim in sides:
        count, length = (lax.axis_size(axis), value.shape[dim])
        up = [(i, (i + 1) % count) for i in range(count - 1)]
        down = [(j, i) for i, j in up]
        last = lax.slice_in_dim(value, length - width, length, axis=dim)
        initial = lax.slice_in_dim(value, 0, width, axis=dim)
        before = lax.ppermute(last, axis, up)
        after = lax.ppermute(initial, axis, down)
        value = jnp.concatenate([before, value, after], axis=dim)
    return value


def from_behind(value, axis, by):
    count = lax.axis_size(axis)
    pairs = [(i, i + by) for i in range(count) if 0 <= i + by < count]
    return lax.ppermute(value, axis, pairs)


def shards(coeffs, kernel, metric, counts, pairs):
    blocks = coeffs.shape[0]
    half = coeffs.shape[1]
    width = coeffs.shape[2]
    here = lax.axis_index("curve")
    core = lax.axis_index("aux")
    window = extended(coeffs, (("curve", 0),), blocks)
    anchor = here * blocks - blocks
    rows = core * half + jnp.arange(half, dtype=jnp.int32)

    def step(index, acc):
        pair = lax.dynamic_index_in_dim(pairs, index, 0, keepdims=False)
        first = pair[0]
        second = pair[1]
        first_slot = first - anchor
        second_slot = second - anchor
        ca = lax.dynamic_index_in_dim(window, first_slot, 0, keepdims=False)
        cb = lax.dynamic_index_in_dim(window, second_slot, 0, keepdims=False)
        kblock = lax.dynamic_index_in_dim(kernel, index, 0, keepdims=False)
        left = jnp.dot(ca, kblock, preferred_element_type=jnp.float32)
        density = jnp.sum(left * cb.astype(jnp.float32), axis=1)
        live = rows < jnp.minimum(counts[first], counts[second])
        metric_first = lax.dynamic_index_in_dim(metric, first, 0, keepdims=False)
        metric_second = lax.dynamic_index_in_dim(metric, second, 0, keepdims=False)
        weight = jnp.where(
            live, metric_first * metric_second * density * NG ** (-0.5), jnp.float32(0.0)
        )
        scaled = (weight[:, None] * cb.astype(jnp.float32)).astype(jnp.bfloat16)
        block = lax.dot_general(
            ca, scaled, (((0,), (0,)), ((), ())), preferred_element_type=jnp.float32
        ) * AUXB ** (-0.5)
        acc = acc.at[first_slot].add(block)
        acc = acc.at[second_slot].add(block.T)
        return acc

    start = jnp.zeros((3 * blocks, width, width), jnp.float32)
    acc = lax.fori_loop(0, pairs.shape[0], step, start)
    from_next = from_behind(acc[:blocks], "curve", -1)
    from_prev = from_behind(acc[2 * blocks :], "curve", 1)
    owned = acc[blocks : 2 * blocks] + from_next + from_prev
    return lax.psum_scatter(owned, "aux", scatter_dimension=1, tiled=True)


def solution(mesh):
    in_specs = (
        P("curve", "aux", None),
        P("curve", None, None),
        P(None, "aux"),
        P(),
        P("curve", None),
    )
    out_specs = P("curve", "aux", None)
    return jax.shard_map(shards, mesh=mesh, in_specs=in_specs, out_specs=out_specs, check_vma=False)
```

profile of v0, /device:TPU:97, one launch (start us, length us, event | category | flops | bytes accessed | tf_op | source)
XLA Modules:
  0.0 481.5 jit_solution(5309061373339120182)
XLA Ops:
  6.5 3.1 collective-permute-start
  9.7 6.4 %collective-permute-start.1 = (bf16[2,6400,320]{1,2,0:T(8,128)(2,1)}, bf16[2,6400,320]{1,2,0:T(8,128)(2,1)}, u32[]{:S(2)}, u32[]{:S(2)}) collective-permute-start(bf16[2,6400,320]{1,2,0:T(8,128)(2,1)} %param.11), channel_id=1, source_target_pairs={{2,0},{4,2},{6,4},{8,6},{10,8},{12,10},{14,12},{16,14},{18,16},{20... | collective-permute-start | bytes 24576008 | tf_op jit(solution)/shard_map/ppermute | solution.py:18
  16.1 174.0 %collective-permute-done = bf16[2,6400,320]{1,2,0:T(8,128)(2,1)} collective-permute-done((bf16[2,6400,320]{1,2,0:T(8,128)(2,1)}, bf16[2,6400,320]{1,2,0:T(8,128)(2,1)}, u32[]{:S(2)}, u32[]{:S(2)}) %collective-permute-start) | collective-permute-done | bytes 8192032 | tf_op jit(solution)/shard_map/ppermute | solution.py:17
  190.1 0.9 collective-permute-done.1
  190.9 20.5 %pad_maximum_fusion = bf16[6,6400,320]{1,2,0:T(8,128)(2,1)} fusion(bf16[2,6400,320]{1,2,0:T(8,128)(2,1)} %collective-permute-done.1, bf16[2,6400,320]{1,2,0:T(8,128)(2,1)} %param.11, bf16[2,6400,320]{1,2,0:T(8,128)(2,1)} %collective-permute-done), kind=kLoop, calls=%fused_computation.33 | loop fusion | flops 24576000 | bytes 49152000 | tf_op jit(solution)/shard_map/concatenate | solution.py:19
  211.5 1.8 broadcast_in_dim.18
  213.3 211.8 %while.16 = (s32[]{:T(128)}, f32[6,320,320]{1,2,0:T(8,128)}, s32[8,2]{0,1:T(2,128)S(1)}, s32[]{:T(128)}, bf16[6,6400,320]{1,2,0:T(8,128)(2,1)}, /*index=5*/s32[1...) while((s32[]{:T(128)}, f32[6,320,320]{1,2,0:T(8,128)}, ...), condition=%wide.region_4.5_spmd.clone, body=%wide.region_0.4_spmd.clone.sunk | while | flops 2634272000 | bytes 20853664 | solution.py:65
  215.2 5.9 %fusion.45 = f32[6400]{0:T(1024)S(1)} fusion(bf16[6,6400,320]{1,2,0:T(8,128)(2,1)} %get-tuple-element.352, s32[]{:T(128)} %select_n.75, s32[]{:T(128)} %select_n.72, bf16[8,320,320]{2,1,0:T(8,128)(2,1)} %get-tuple-element.355, s32[]{:T(128)} %get-tuple-element.333), kind=kOutput, calls=%fused_computation.13.clone.1 | convolution fusion | flops 1316857600 | bytes 8464896 | tf_op jit(solution)/shard_map/while/body/eval_jaxpr/dot_general | solution.py:48
  226.8 1.1 multiply_reduce_fusion.2
  228.0 5.7 %fusion.47 = f32[320,320]{1,0:T(8,128)S(1)} fusion(f32[6400]{0:T(1024)S(1)} %multiply_select_fusion.2, bf16[6,6400,320]{1,2,0:T(8,128)(2,1)} %get-tuple-element.352, s32[]{:T(128)} %select_n.75, s32[]{:T(128)} %select_n.72), kind=kOutput, calls=%fused_computation.14.clone.1 | convolution fusion | flops 1316966400 | bytes 8628224 | tf_op jit(solution)/shard_map/while/body/eval_jaxpr/dot_general | solution.py:57
  233.9 0.7 and_reduce_fusion.3
  234.6 2.6 fusion.48
  237.3 2.5 fusion.49
  241.7 5.9 %fusion.45 = f32[6400]{0:T(1024)S(1)} fusion(bf16[6,6400,320]{1,2,0:T(8,128)(2,1)} %get-tuple-element.352, s32[]{:T(128)} %select_n.75, s32[]{:T(128)} %select_n.72, bf16[8,320,320]{2,1,0:T(8,128)(2,1)} %get-tuple-element.355, s32[]{:T(128)} %get-tuple-element.333), kind=kOutput, calls=%fused_computation.13.clone.1 | convolution fusion | flops 1316857600 | bytes 8464896 | tf_op jit(solution)/shard_map/while/body/eval_jaxpr/dot_general | solution.py:48
  251.4 0.6 fusion.46
  253.3 1.1 multiply_reduce_fusion.2
  254.4 5.7 %fusion.47 = f32[320,320]{1,0:T(8,128)S(1)} fusion(f32[6400]{0:T(1024)S(1)} %multiply_select_fusion.2, bf16[6,6400,320]{1,2,0:T(8,128)(2,1)} %get-tuple-element.352, s32[]{:T(128)} %select_n.75, s32[]{:T(128)} %select_n.72), kind=kOutput, calls=%fused_computation.14.clone.1 | convolution fusion | flops 1316966400 | bytes 8628224 | tf_op jit(solution)/shard_map/while/body/eval_jaxpr/dot_general | solution.py:57
  260.4 0.7 and_reduce_fusion.3
  261.1 2.6 fusion.48
  263.7 2.5 fusion.49
  268.1 5.9 %fusion.45 = f32[6400]{0:T(1024)S(1)} fusion(bf16[6,6400,320]{1,2,0:T(8,128)(2,1)} %get-tuple-element.352, s32[]{:T(128)} %select_n.75, s32[]{:T(128)} %select_n.72, bf16[8,320,320]{2,1,0:T(8,128)(2,1)} %get-tuple-element.355, s32[]{:T(128)} %get-tuple-element.333), kind=kOutput, calls=%fused_computation.13.clone.1 | convolution fusion | flops 1316857600 | bytes 8464896 | tf_op jit(solution)/shard_map/while/body/eval_jaxpr/dot_general | solution.py:48
  277.8 0.6 fusion.46
  279.7 1.1 multiply_reduce_fusion.2
  280.9 5.7 %fusion.47 = f32[320,320]{1,0:T(8,128)S(1)} fusion(f32[6400]{0:T(1024)S(1)} %multiply_select_fusion.2, bf16[6,6400,320]{1,2,0:T(8,128)(2,1)} %get-tuple-element.352, s32[]{:T(128)} %select_n.75, s32[]{:T(128)} %select_n.72), kind=kOutput, calls=%fused_computation.14.clone.1 | convolution fusion | flops 1316966400 | bytes 8628224 | tf_op jit(solution)/shard_map/while/body/eval_jaxpr/dot_general | solution.py:57
  286.8 0.7 and_reduce_fusion.3
  287.5 2.6 fusion.48
  290.1 2.6 fusion.49
  294.5 5.9 %fusion.45 = f32[6400]{0:T(1024)S(1)} fusion(bf16[6,6400,320]{1,2,0:T(8,128)(2,1)} %get-tuple-element.352, s32[]{:T(128)} %select_n.75, s32[]{:T(128)} %select_n.72, bf16[8,320,320]{2,1,0:T(8,128)(2,1)} %get-tuple-element.355, s32[]{:T(128)} %get-tuple-element.333), kind=kOutput, calls=%fused_computation.13.clone.1 | convolution fusion | flops 1316857600 | bytes 8464896 | tf_op jit(solution)/shard_map/while/body/eval_jaxpr/dot_general | solution.py:48
  306.1 1.1 multiply_reduce_fusion.2
  307.3 5.7 %fusion.47 = f32[320,320]{1,0:T(8,128)S(1)} fusion(f32[6400]{0:T(1024)S(1)} %multiply_select_fusion.2, bf16[6,6400,320]{1,2,0:T(8,128)(2,1)} %get-tuple-element.352, s32[]{:T(128)} %select_n.75, s32[]{:T(128)} %select_n.72), kind=kOutput, calls=%fused_computation.14.clone.1 | convolution fusion | flops 1316966400 | bytes 8628224 | tf_op jit(solution)/shard_map/while/body/eval_jaxpr/dot_general | solution.py:57
  313.2 0.7 and_reduce_fusion.3
  314.0 2.6 fusion.48
  316.6 2.6 fusion.49
  321.0 5.9 %fusion.45 = f32[6400]{0:T(1024)S(1)} fusion(bf16[6,6400,320]{1,2,0:T(8,128)(2,1)} %get-tuple-element.352, s32[]{:T(128)} %select_n.75, s32[]{:T(128)} %select_n.72, bf16[8,320,320]{2,1,0:T(8,128)(2,1)} %get-tuple-element.355, s32[]{:T(128)} %get-tuple-element.333), kind=kOutput, calls=%fused_computation.13.clone.1 | convolution fusion | flops 1316857600 | bytes 8464896 | tf_op jit(solution)/shard_map/while/body/eval_jaxpr/dot_general | solution.py:48
  332.6 1.1 multiply_reduce_fusion.2
  333.8 5.7 %fusion.47 = f32[320,320]{1,0:T(8,128)S(1)} fusion(f32[6400]{0:T(1024)S(1)} %multiply_select_fusion.2, bf16[6,6400,320]{1,2,0:T(8,128)(2,1)} %get-tuple-element.352, s32[]{:T(128)} %select_n.75, s32[]{:T(128)} %select_n.72), kind=kOutput, calls=%fused_computation.14.clone.1 | convolution fusion | flops 1316966400 | bytes 8628224 | tf_op jit(solution)/shard_map/while/body/eval_jaxpr/dot_general | solution.py:57
  339.7 0.7 and_reduce_fusion.3
  340.4 2.6 fusion.48
  343.0 2.6 fusion.49
  347.5 5.9 %fusion.45 = f32[6400]{0:T(1024)S(1)} fusion(bf16[6,6400,320]{1,2,0:T(8,128)(2,1)} %get-tuple-element.352, s32[]{:T(128)} %select_n.75, s32[]{:T(128)} %select_n.72, bf16[8,320,320]{2,1,0:T(8,128)(2,1)} %get-tuple-element.355, s32[]{:T(128)} %get-tuple-element.333), kind=kOutput, calls=%fused_computation.13.clone.1 | convolution fusion | flops 1316857600 | bytes 8464896 | tf_op jit(solution)/shard_map/while/body/eval_jaxpr/dot_general | solution.py:48
  359.1 1.1 multiply_reduce_fusion.2
  360.2 5.7 %fusion.47 = f32[320,320]{1,0:T(8,128)S(1)} fusion(f32[6400]{0:T(1024)S(1)} %multiply_select_fusion.2, bf16[6,6400,320]{1,2,0:T(8,128)(2,1)} %get-tuple-element.352, s32[]{:T(128)} %select_n.75, s32[]{:T(128)} %select_n.72), kind=kOutput, calls=%fused_computation.14.clone.1 | convolution fusion | flops 1316966400 | bytes 8628224 | tf_op jit(solution)/shard_map/while/body/eval_jaxpr/dot_general | solution.py:57
  366.2 0.7 and_reduce_fusion.3
  366.9 2.6 fusion.48
  369.5 2.6 fusion.49
  374.0 5.9 %fusion.45 = f32[6400]{0:T(1024)S(1)} fusion(bf16[6,6400,320]{1,2,0:T(8,128)(2,1)} %get-tuple-element.352, s32[]{:T(128)} %select_n.75, s32[]{:T(128)} %select_n.72, bf16[8,320,320]{2,1,0:T(8,128)(2,1)} %get-tuple-element.355, s32[]{:T(128)} %get-tuple-element.333), kind=kOutput, calls=%fused_computation.13.clone.1 | convolution fusion | flops 1316857600 | bytes 8464896 | tf_op jit(solution)/shard_map/while/body/eval_jaxpr/dot_general | solution.py:48
  385.6 1.1 multiply_reduce_fusion.2
  386.8 5.7 %fusion.47 = f32[320,320]{1,0:T(8,128)S(1)} fusion(f32[6400]{0:T(1024)S(1)} %multiply_select_fusion.2, bf16[6,6400,320]{1,2,0:T(8,128)(2,1)} %get-tuple-element.352, s32[]{:T(128)} %select_n.75, s32[]{:T(128)} %select_n.72), kind=kOutput, calls=%fused_computation.14.clone.1 | convolution fusion | flops 1316966400 | bytes 8628224 | tf_op jit(solution)/shard_map/while/body/eval_jaxpr/dot_general | solution.py:57
  392.7 0.7 and_reduce_fusion.3
  393.4 2.6 fusion.48
  396.0 2.6 fusion.49
  400.5 5.9 %fusion.45 = f32[6400]{0:T(1024)S(1)} fusion(bf16[6,6400,320]{1,2,0:T(8,128)(2,1)} %get-tuple-element.352, s32[]{:T(128)} %select_n.75, s32[]{:T(128)} %select_n.72, bf16[8,320,320]{2,1,0:T(8,128)(2,1)} %get-tuple-element.355, s32[]{:T(128)} %get-tuple-element.333), kind=kOutput, calls=%fused_computation.13.clone.1 | convolution fusion | flops 1316857600 | bytes 8464896 | tf_op jit(solution)/shard_map/while/body/eval_jaxpr/dot_general | solution.py:48
  412.1 1.1 multiply_reduce_fusion.2
  413.3 5.7 %fusion.47 = f32[320,320]{1,0:T(8,128)S(1)} fusion(f32[6400]{0:T(1024)S(1)} %multiply_select_fusion.2, bf16[6,6400,320]{1,2,0:T(8,128)(2,1)} %get-tuple-element.352, s32[]{:T(128)} %select_n.75, s32[]{:T(128)} %select_n.72), kind=kOutput, calls=%fused_computation.14.clone.1 | convolution fusion | flops 1316966400 | bytes 8628224 | tf_op jit(solution)/shard_map/while/body/eval_jaxpr/dot_general | solution.py:57
  419.2 0.7 and_reduce_fusion.3
  419.9 2.6 fusion.48
  422.5 2.6 fusion.49
  425.1 2.4 copy.10
  427.7 8.1 %collective-permute-start.2 = (f32[2,320,320]{2,1,0:T(8,128)S(1)}, f32[2,320,320]{2,1,0:T(8,128)S(1)}, u32[]{:S(2)}, u32[]{:S(2)}) collective-permute-start(f32[2,320,320]{2,1,0:T(8,128)S(1)} %get-tuple-element.249), channel_id=1, source_target_pairs={{2,0},{4,2},{6,4},{8,6},{10,8},{12,10},{14,12},{16,14},{18,16},{20... | collective-permute-start | bytes 2457608 | tf_op jit(solution)/shard_map/ppermute | solution.py:26
  435.8 1.9 collective-permute-start.3
  437.7 17.2 %collective-permute-done.2 = f32[2,320,320]{2,1,0:T(8,128)S(1)} collective-permute-done((f32[2,320,320]{2,1,0:T(8,128)S(1)}, f32[2,320,320]{2,1,0:T(8,128)S(1)}, u32[]{:S(2)}, u32[]{:S(2)}) %collective-permute-start.2) | collective-permute-done | bytes 819232 | tf_op jit(solution)/shard_map/ppermute | solution.py:26
  454.9 8.1 %collective-permute-done.3 = f32[2,320,320]{2,1,0:T(8,128)S(1)} collective-permute-done((f32[2,320,320]{2,1,0:T(8,128)S(1)}, f32[2,320,320]{2,1,0:T(8,128)S(1)}, u32[]{:S(2)}, u32[]{:S(2)}) %collective-permute-start.3) | collective-permute-done | bytes 819232 | tf_op jit(solution)/shard_map/ppermute | solution.py:26
  463.0 1.2 fusion.26
  464.2 10.5 %reduce-scatter.2.cloned.1.call-done = f32[2,160,320]{2,1,0:T(8,128)} async-done(((f32[2,320,320]{2,1,0:T(8,128)}), f32[2,160,320]{2,1,0:T(8,128)}) %reduce-scatter.2.cloned.1.call-update) | async-done | bytes 409616 | tf_op jit(solution)/shard_map/reduce_scatter | solution.py:69
  (47 shorter events, 10.6 us)
Async XLA Ops:
  6.5 468.1 %reduce-scatter.2.cloned.1.call-start = ((), (), s32[]{:S(2)}) async-start(), calls=%async_computation.1 | async-start | bytes 1474560 | tf_op jit(solution)/shard_map/reduce_scatter | solution.py:69
  6.5 183.5 %collective-permute-start = (bf16[2,6400,320]{1,2,0:T(8,128)(2,1)}, bf16[2,6400,320]{1,2,0:T(8,128)(2,1)}, u32[]{:S(2)}, u32[]{:S(2)}) collective-permute-start(bf16[2,6400,320]{1,2,0:T(8,128)(2,1)} %param.11), channel_id=1, source_target_pairs={{0,2},{2,4},{4,6},{6,8},{8,10},{10,12},{12,14},{14,16},{16,18},{18... | collective-permute-start | bytes 24576008 | tf_op jit(solution)/shard_map/ppermute | solution.py:17
  9.7 181.3 %collective-permute-start.1 = (bf16[2,6400,320]{1,2,0:T(8,128)(2,1)}, bf16[2,6400,320]{1,2,0:T(8,128)(2,1)}, u32[]{:S(2)}, u32[]{:S(2)}) collective-permute-start(bf16[2,6400,320]{1,2,0:T(8,128)(2,1)} %param.11), channel_id=1, source_target_pairs={{2,0},{4,2},{6,4},{8,6},{10,8},{12,10},{14,12},{16,14},{18,16},{20... | collective-permute-start | bytes 24576008 | tf_op jit(solution)/shard_map/ppermute | solution.py:18
  16.1 197.3 %copy-start = (s32[128]{0:T(128)S(1)}, s32[128]{0:T(128)}, u32[]{:S(2)}) copy-start(s32[128]{0:T(128)} %param.14) | copy-start | bytes 1540
  16.1 197.2 %copy-start.1 = (s32[8,2]{0,1:T(2,128)S(1)}, s32[8,2]{0,1:T(2,128)}, u32[]{:S(2)}) copy-start(s32[8,2]{0,1:T(2,128)} %param.15) | copy-start | bytes 196
  16.1 197.2 %copy-start.2 = (s32[3]{0:T(128)S(1)}, s32[3]{0:T(128)}, u32[]{:S(2)}) copy-start(s32[3]{0:T(128)} %constant.152.clone.2) | copy-start | bytes 40
  427.7 27.2 %collective-permute-start.2 = (f32[2,320,320]{2,1,0:T(8,128)S(1)}, f32[2,320,320]{2,1,0:T(8,128)S(1)}, u32[]{:S(2)}, u32[]{:S(2)}) collective-permute-start(f32[2,320,320]{2,1,0:T(8,128)S(1)} %get-tuple-element.249), channel_id=1, source_target_pairs={{2,0},{4,2},{6,4},{8,6},{10,8},{12,10},{14,12},{16,14},{18,16},{20... | collective-permute-start | bytes 2457608 | tf_op jit(solution)/shard_map/ppermute | solution.py:26
  435.8 27.2 %collective-permute-start.3 = (f32[2,320,320]{2,1,0:T(8,128)S(1)}, f32[2,320,320]{2,1,0:T(8,128)S(1)}, u32[]{:S(2)}, u32[]{:S(2)}) collective-permute-start(f32[2,320,320]{2,1,0:T(8,128)S(1)} %get-tuple-element.250), channel_id=1, source_target_pairs={{0,2},{2,4},{4,6},{6,8},{8,10},{10,12},{12,14},{14,16},{16,18},{18... | collective-permute-start | bytes 2457608 | tf_op jit(solution)/shard_map/ppermute | solution.py:26
Sparse Core Ops, SparseCore 0:
  464.3 10.3 reduce-scatter.1
where the time goes:
time: 486 us; the launch traced here: 482 us
  waiting for transfers between devices  211 us (43%)
  matrix products  93 us (19%)
  other arithmetic  78 us (16%)
  loops' own time  51 us (10%)
  starting transfers between devices  19.5 us (4%)
  local copies, waits for them, and re-layouts  15.9 us (3%)
  between operations  13.5 us (3%)
    ppermute x1, waiting for transfers between devices, extended(): before = lax.ppermute(last, axis, up)  174 us
    another operation x1, loops' own time, shards(): acc = lax.fori_loop(0, pairs.shape[0], step, start)  51 us
    dot_general x8, matrix products, step(): left = jnp.dot(ca, kblock, preferred_element_type=jnp.float32)  47.3 us
    dot_general x8, matrix products, step(): lax.dot_general(ca, scaled, (((0,), (0,)), ((), ())), preferred_element_t...  45.7 us
    ppermute x2, waiting for transfers between devices, from_behind(): return lax.ppermute(value, axis, pairs)  25.3 us
    scatter-add x8, other arithmetic, step(): acc = acc.at[first_slot].add(block)  20.7 us
    scatter-add x8, other arithmetic, step(): acc = acc.at[second_slot].add(block.T)  20.6 us
    concatenate x1, other arithmetic, extended(): value = jnp.concatenate([before, value, after], axis=dim)  20.5 us
  transfers between devices with their start and end apart: 5, of which 5 were waited for; matrix products, arithmetic and copies ran while one was open for 0% of the time, Pallas kernels for 0%

commit v1 on v0

v1 whole, which is shorter than its diff:
```python
import functools

import jax
import jax.numpy as jnp
from jax import lax
from jax.experimental import pallas as pl
from jax.experimental.pallas import tpu as pltpu
from jax.sharding import PartitionSpec as P

MESH = pl.DeviceIdType.MESH
NG = 320
AUXB = 12800
ROWS = 6400
HALF = 3200
PART = 640
PARTS = HALF // PART
PAIRS = 8
RING = 64
NBLK = 128
OUT = NG // 2
F32 = jnp.float32
BF16 = jnp.bfloat16


def across(a, b):
    return lax.dot_general(a, b, (((1,), (1,)), ((), ())), preferred_element_type=F32)


def body(
    coeffs, kernel, metric, counts, pairs, out,
    own, got, blocks, met, sums, sent_k, got_k, mix, mix_own, weight_own, zs, acc,
    got_pair, send_res, got_res,
    load_sem, row_send, row_recv, k_send, k_recv, kf_send, kf_recv,
    pair_send, pair_recv, res_send, res_recv,
):
    here = lax.axis_index("curve")
    core = lax.axis_index("aux")
    after = lax.rem(here + 1, RING)
    before = lax.rem(here + RING - 1, RING)
    sides = ((before, core), (after, core))
    twin = (here, 1 - core)

    barrier = pltpu.get_barrier_semaphore()
    for target in (*sides, twin):
        pl.semaphore_signal(barrier, inc=1, device_id=target, device_id_type=MESH)

    loads = [
        pltpu.make_async_copy(kernel, blocks, load_sem.at[0]),
        pltpu.make_async_copy(metric, met, load_sem.at[1]),
        pltpu.make_async_copy(coeffs, own, load_sem.at[2]),
    ]
    for load in loads:
        load.start()
    loads[0].wait()

    first = [pairs[p, 0] - 2 * here for p in range(PAIRS)]
    second = [pairs[p, 1] - 2 * here + 2 for p in range(PAIRS)]

    def add_kernels(index, _):
        i = index // 6
        s = index % 6
        named = [(first[p] == i) & (second[p] == s) for p in range(PAIRS)]

        def rows(r, _):
            at = pl.ds(pl.multiple_of(r * 64, 64), 64)
            total = jnp.zeros((64, NG), F32)
            for p in range(PAIRS):
                total = total + jnp.where(named[p], blocks[p, at, :].astype(F32), 0.0)
            sums[index, at, :] = total
            return 0

        return lax.fori_loop(0, NG // 64, rows, 0)

    lax.fori_loop(0, 12, add_kernels, 0)

    for e in range(2):
        for j in range(2):
            sent_k[e, j] = sums[6 * core + 4 * e + j].astype(BF16)

    pl.semaphore_wait(barrier, 3)

    def k_copy(e):
        return pltpu.make_async_remote_copy(
            src_ref=sent_k.at[e],
            dst_ref=got_k.at[1 - e, core],
            send_sem=k_send.at[e],
            recv_sem=k_recv.at[1 - e],
            device_id=sides[e],
            device_id_type=MESH,
        )

    def k_forward(e):
        return pltpu.make_async_remote_copy(
            src_ref=got_k.at[e, core],
            dst_ref=got_k.at[e, core],
            send_sem=kf_send.at[e],
            recv_sem=kf_recv.at[e],
            device_id=twin,
            device_id_type=MESH,
        )

    def row_copy(e, k):
        start = (1 - e) * HALF if e == 0 else 0
        start = start + k * PART
        at = pl.ds(pl.multiple_of(start, 128), PART)
        to = pl.ds(pl.multiple_of(k * PART, 128), PART)
        return pltpu.make_async_remote_copy(
            src_ref=coeffs.at[:, :, at],
            dst_ref=got.at[1 - e, :, :, to],
            send_sem=row_send.at[e, k],
            recv_sem=row_recv.at[1 - e, k],
            device_id=sides[e],
            device_id_type=MESH,
        )

    def row_wait(e, k):
        row_copy(1 - e, k).wait_recv()

    for e in range(2):
        k_copy(e).start()
    for k in range(2):
        for e in range(2):
            row_copy(e, k).start()

    eye = (
        lax.broadcasted_iota(jnp.int32, (NG, NG), 0)
        == lax.broadcasted_iota(jnp.int32, (NG, NG), 1)
    ).astype(BF16)
    loads[1].wait()
    loads[2].wait()
    mix_own[0] = sums[2].astype(BF16)
    mix_own[2] = sums[9].astype(BF16)
    mix_own[1] = (sums[3] + across(eye, sums[8].astype(BF16))).astype(BF16)

    block_of = [lax.rem(2 * here + NBLK - 2 + s, NBLK) for s in range(6)]
    count_of = [counts[block_of[s]] for s in range(6)]

    def factor(s, t, start, size):
        at = pl.ds(pl.multiple_of(start, 128), size)
        a = met[pl.ds(block_of[s], 1), at]
        b = met[pl.ds(block_of[t], 1), at]
        row = core * ROWS + start + lax.broadcasted_iota(jnp.int32, (1, size), 1)
        live = row < jnp.minimum(count_of[s], count_of[t])
        return live, a * b * NG ** (-0.5)

    def own_part(k, _):
        start = pl.multiple_of(k * PART, 128)
        at = pl.ds(start, PART)
        for index, (i, j) in enumerate(((0, 0), (0, 1), (1, 1))):
            left = jnp.dot(mix_own[index], own[j, :, at], preferred_element_type=F32)
            density = jnp.sum(left * own[i, :, at].astype(F32), axis=0, keepdims=True)
            live, scale = factor(2 + i, 2 + j, start, PART)
            weight_own[pl.ds(index, 1), at] = jnp.where(live, scale * density, 0.0)
        return 0

    lax.fori_loop(0, ROWS // PART, own_part, 0)

    for e in range(2):
        k_copy(1 - e).wait_recv()
        k_forward(e).start()
    for e in range(2):
        pltpu.make_async_remote_copy(
            src_ref=got_k.at[e, core],
            dst_ref=got_k.at[e, 1 - core],
            send_sem=kf_send.at[e],
            recv_sem=kf_recv.at[e],
            device_id=twin,
            device_id_type=MESH,
        ).wait_recv()
        for j in range(2):
            for i in range(2):
                turned = across(eye, got_k[e, j, i])
                mix[e, j, i * NG:(i + 1) * NG, :] = (sums[6 * i + 4 * e + j] + turned).astype(BF16)

    acc[...] = jnp.zeros_like(acc)

    def put(slot, value):
        high = value.astype(BF16)
        zs[slot, 0] = high
        zs[slot, 1] = (value - high.astype(F32)).astype(BF16)

    def edge(e, k):
        start = e * HALF + k * PART
        at = pl.ds(pl.multiple_of(start, 128), PART)
        to = pl.ds(pl.multiple_of(k * PART, 128), PART)
        y = [own[i, :, at].astype(F32) for i in range(2)]
        weights = []
        for j in range(2):
            left = jnp.dot(mix[e, j], got[e, j, :, to], preferred_element_type=F32)
            each = []
            for i in range(2):
                density = jnp.sum(left[i * NG:(i + 1) * NG] * y[i], axis=0, keepdims=True)
                live, scale = factor(2 + i, 4 * e + j, start, PART)
                each.append(jnp.where(live, scale * density, 0.0))
            weights.append(each)
        mine = [weight_own[pl.ds(index, 1), at] for index in range(3)]
        x = [got[e, j, :, to].astype(F32) for j in range(2)]
        put(0, weights[0][0] * x[0] + weights[1][0] * x[1] + 2.0 * mine[0] * y[0] + mine[1] * y[1])
        put(1, weights[0][1] * x[0] + weights[1][1] * x[1] + mine[1] * y[0] + 2.0 * mine[2] * y[1])
        for j in range(2):
            put(2 + j, weights[j][0] * y[0] + weights[j][1] * y[1])
        for i in range(2):
            rows = own[i, :, at]
            acc[i] += across(rows, zs[i, 0]) + across(rows, zs[i, 1])
        for j in range(2):
            rows = got[e, j, :, to]
            acc[2 + 2 * e + j] += across(rows, zs[2 + j, 0]) + across(rows, zs[2 + j, 1])

    def step(k, _):
        for e in range(2):
            row_copy(e, k).wait_send()

            @pl.when(k + 2 < PARTS)
            def _():
                row_copy(e, k + 2).start()

        for e in range(2):
            row_wait(e, k)
            edge(e, k)
        return 0

    lax.fori_loop(0, PARTS, step, 0)

    keep = pl.ds(pl.multiple_of(core * OUT, 32), OUT)
    give = pl.ds(pl.multiple_of((1 - core) * OUT, 32), OUT)
    order = ((2, 2), (4, 2), (0, 2))
    swaps = [
        pltpu.make_async_remote_copy(
            src_ref=acc.at[pl.ds(start, size), give],
            dst_ref=got_pair.at[pl.ds(start, size)],
            send_sem=pair_send.at[n],
            recv_sem=pair_recv.at[n],
            device_id=twin,
            device_id_type=MESH,
        )
        for n, (start, size) in enumerate(order)
    ]
    for swap in swaps:
        swap.start()
    results = [
        pltpu.make_async_remote_copy(
            src_ref=send_res.at[e],
            dst_ref=got_res.at[1 - e],
            send_sem=res_send.at[e],
            recv_sem=res_recv.at[1 - e],
            device_id=sides[e],
            device_id_type=MESH,
        )
        for e in range(2)
    ]
    norm = AUXB ** (-0.5)
    for e in range(2):
        swaps[e].wait_recv()
        for j in range(2):
            total = acc[2 + 2 * e + j, keep, :] + got_pair[2 + 2 * e + j]
            send_res[e, j] = (total * norm).astype(BF16)
        results[e].start()
    swaps[2].wait_recv()
    for i in range(2):
        out[i] = (acc[i, keep, :] + got_pair[i]) * norm
    for e in range(2):
        results[1 - e].wait_recv()
        for i in range(2):
            out[i] += got_res[e, i].astype(F32)
    for e in range(2):
        k_copy(e).wait_send()
        k_forward(e).wait_send()
        results[e].wait_send()
    for swap in swaps:
        swap.wait_send()


def shards(coeffs, kernel, metric, counts, pairs):
    anywhere = pl.BlockSpec(memory_space=pl.ANY)
    scalars = pl.BlockSpec(memory_space=pltpu.SMEM)
    dma = pltpu.SemaphoreType.DMA
    return pl.pallas_call(
        body,
        out_shape=jax.ShapeDtypeStruct((2, OUT, NG), F32),
        in_specs=[anywhere, anywhere, anywhere, scalars, scalars],
        out_specs=pl.BlockSpec(memory_space=pltpu.VMEM),
        scratch_shapes=[
            pltpu.VMEM((2, NG, ROWS), BF16),
            pltpu.VMEM((2, 2, NG, HALF), BF16),
            pltpu.VMEM((PAIRS, NG, NG), BF16),
            pltpu.VMEM((NBLK, ROWS), F32),
            pltpu.VMEM((12, NG, NG), F32),
            pltpu.VMEM((2, 2, NG, NG), BF16),
            pltpu.VMEM((2, 2, 2, NG, NG), BF16),
            pltpu.VMEM((2, 2, 2 * NG, NG), BF16),
            pltpu.VMEM((3, NG, NG), BF16),
            pltpu.VMEM((8, ROWS), F32),
            pltpu.VMEM((4, 2, NG, PART), BF16),
            pltpu.VMEM((6, NG, NG), F32),
            pltpu.VMEM((6, OUT, NG), F32),
            pltpu.VMEM((2, 2, OUT, NG), BF16),
            pltpu.VMEM((2, 2, OUT, NG), BF16),
            dma((3,)),
            dma((2, PARTS)),
            dma((2, PARTS)),
            dma((2,)),
            dma((2,)),
            dma((2,)),
            dma((2,)),
            dma((3,)),
            dma((3,)),
            dma((2,)),
            dma((2,)),
        ],
        compiler_params=pltpu.CompilerParams(
            collective_id=0, has_side_effects=True, vmem_limit_bytes=58 * 2 ** 20
        ),
        cost_estimate=pl.CostEstimate(
            flops=30 * 10 ** 9, bytes_accessed=14 * 10 ** 6, transcendentals=0
        ),
    )(jnp.transpose(coeffs, (0, 2, 1)), kernel, metric, counts, pairs)


def solution(mesh):
    in_specs = (
        P("curve", "aux", None),
        P("curve", None, None),
        P(None, "aux"),
        P(),
        P("curve", None),
    )
    out_specs = P("curve", "aux", None)
    return jax.shard_map(shards, mesh=mesh, in_specs=in_specs, out_specs=out_specs, check_vma=False)
```

time: 486 us -> 139 us (0.29)
  the two profiles are of different devices: /device:TPU:97 before, /device:TPU:1 now
where the time goes in v1:
time: 139 us
  Pallas kernels  136 us (98%)
  local copies, waits for them, and re-layouts  3.19 us (2%)
    pallas_call x1, Pallas kernels, shards(): pl.pallas_call(body, out_shape=jax.ShapeDtypeStruct((2, OUT, NG), F32), i...  136 us
    unnamed x2, local copies, waits for them, and re-layouts  3.19 us

profile of v1, /device:TPU:1, one launch (start us, length us, event | category | flops | bytes accessed | tf_op | source)
XLA Modules:
  0.0 139.0 jit_solution(6246844176210704587)
XLA Ops:
  0.0 1.3 copy.6.pairs
  1.3 135.8 %shard_map.55 = f32[2,160,320]{2,1,0:T(8,128)} custom-call(bf16[2,320,6400]{2,1,0:T(8,128)(2,1)} %bitcast.1, bf16[8,320,320]{2,1,0:T(8,128)(2,1)} %kernel.1, f32[128,6400]{1,0:T(8,128)} %metric.1, s32[128]{0:T(128)} %counts.1, s32[8,2]{1,0:T(8,128)} %copy.6.pairs), custom_call_target="tpu_custom_call" | custom-call | flops 30000001024 | bytes 14000000 | tf_op jit(solution)/shard_map/pallas_call | solution.py:277
  137.1 1.8 %copy.8 = f32[2,160,320]{2,1,0:T(8,128)} copy(f32[2,160,320]{2,1,0:T(8,128)} %shard_map.55) | data formatting | bytes 819200

commit v2 on v1

v2 whole, which is shorter than its diff:
```python
import functools

import jax
import jax.numpy as jnp
from jax import lax
from jax.experimental import pallas as pl
from jax.experimental.pallas import tpu as pltpu
from jax.sharding import PartitionSpec as P

MESH = pl.DeviceIdType.MESH
NG = 320
AUXB = 12800
ROWS = 6400
BOTH = 256
ONE = (ROWS - BOTH) // 2
PART = 512
PARTS = 5
OWN_PART = 640
LAST = (384, 128)
SIZES = (PART,) * PARTS + LAST + (BOTH,)
STARTS = tuple(sum(SIZES[:k]) for k in range(len(SIZES)))
COPIES = len(SIZES)
PAIRS = 8
RING = 64
NBLK = 128
OUT = NG // 2
F32 = jnp.float32
BF16 = jnp.bfloat16


def across(a, b):
    return lax.dot_general(a, b, (((1,), (1,)), ((), ())), preferred_element_type=F32)


def body(
    coeffs, kernel, metric, counts, pairs, out,
    own, got, blocks, met, near, sums, sent_k, got_k, mix, mix_own, weight_own, zs, acc,
    got_pair, send_res, got_res,
    load_sem, row_send, row_recv, k_send, k_recv, kf_send, kf_recv,
    pair_send, pair_recv, res_send, res_recv,
):
    here = lax.axis_index("curve")
    core = lax.axis_index("aux")
    after = lax.rem(here + 1, RING)
    before = lax.rem(here + RING - 1, RING)
    sides = ((before, core), (after, core))
    twin = (here, 1 - core)

    barrier = pltpu.get_barrier_semaphore()
    for target in (*sides, twin):
        pl.semaphore_signal(barrier, inc=1, device_id=target, device_id_type=MESH)

    loads = [
        pltpu.make_async_copy(kernel, blocks, load_sem.at[0]),
        pltpu.make_async_copy(metric, met, load_sem.at[1]),
        pltpu.make_async_copy(coeffs, own, load_sem.at[2]),
    ]
    for load in loads:
        load.start()
    pl.semaphore_wait(barrier, 3)

    def k_copy(e):
        return pltpu.make_async_remote_copy(
            src_ref=sent_k.at[e],
            dst_ref=got_k.at[1 - e, core],
            send_sem=k_send.at[e],
            recv_sem=k_recv.at[1 - e],
            device_id=sides[e],
            device_id_type=MESH,
        )

    def k_forward(e):
        return pltpu.make_async_remote_copy(
            src_ref=got_k.at[e, core],
            dst_ref=got_k.at[e, core],
            send_sem=kf_send.at[e],
            recv_sem=kf_recv.at[e],
            device_id=twin,
            device_id_type=MESH,
        )

    def there(e, start):
        if isinstance(start, int):
            return start + (ONE + BOTH) * (e == 1 and start < ONE)
        return pl.multiple_of(start + (ONE + BOTH) * e, 128)

    def row_copy(e, k):
        if isinstance(k, int):
            start, size = STARTS[k], SIZES[k]
        else:
            start, size = pl.multiple_of(k * PART, 128), PART
        return pltpu.make_async_remote_copy(
            src_ref=coeffs.at[:, :, pl.ds(there(1 - e, start), size)],
            dst_ref=got.at[1 - e, :, :, pl.ds(start, size)],
            send_sem=row_send.at[e, k],
            recv_sem=row_recv.at[1 - e, k],
            device_id=sides[e],
            device_id_type=MESH,
        )

    for e in range(2):
        row_copy(e, 0).start()
    loads[0].wait()

    first = [pairs[0, p] - 2 * here for p in range(PAIRS)]
    second = [pairs[1, p] - 2 * here + 2 for p in range(PAIRS)]

    def add_kernels(index, _):
        i = index // 6
        s = index % 6
        named = [(first[p] == i) & (second[p] == s) for p in range(PAIRS)]

        def rows(r, _):
            at = pl.ds(pl.multiple_of(r * 64, 64), 64)
            total = jnp.zeros((64, NG), F32)
            for p in range(PAIRS):
                total = total + jnp.where(named[p], blocks[p, at, :].astype(F32), 0.0)
            sums[index, at, :] = total
            return 0

        return lax.fori_loop(0, NG // 64, rows, 0)

    lax.fori_loop(0, 12, add_kernels, 0)


    for e in range(2):
        both = [sums[6 * core + 4 * e + j].astype(BF16) for j in range(2)]
        sent_k[e] = jnp.concatenate(both, axis=1)
        k_copy(e).start()
    for e in range(2):
        row_copy(e, 1).start()

    wide_eye = (
        lax.broadcasted_iota(jnp.int32, (2 * NG, 2 * NG), 0)
        == lax.broadcasted_iota(jnp.int32, (2 * NG, 2 * NG), 1)
    ).astype(BF16)
    eye = wide_eye[:NG, :NG]
    loads[1].wait()
    loads[2].wait()
    mix_own[0] = sums[2].astype(BF16)
    mix_own[2] = sums[9].astype(BF16)
    mix_own[1] = (sums[3] + across(eye, sums[8].astype(BF16))).astype(BF16)

    block_of = [lax.rem(2 * here + NBLK - 2 + s, NBLK) for s in range(6)]
    count_of = [counts[block_of[s]] for s in range(6)]
    for s in range(6):
        near[s:s + 1, :] = met[pl.ds(block_of[s], 1), :]

    def factor(s, t, start, size):
        at = pl.ds(pl.multiple_of(start, 128), size)
        a = near[s:s + 1, at]
        b = near[t:t + 1, at]
        row = core * ROWS + start + lax.broadcasted_iota(jnp.int32, (1, size), 1)
        live = row < jnp.minimum(count_of[s], count_of[t])
        return live, a * b * NG ** (-0.5)

    def own_part(k, _):
        start = pl.multiple_of(k * OWN_PART, 128)
        at = pl.ds(start, OWN_PART)
        for index, (i, j) in enumerate(((0, 0), (0, 1), (1, 1))):
            left = jnp.dot(mix_own[index], own[j, :, at], preferred_element_type=F32)
            density = jnp.sum(left * own[i, :, at].astype(F32), axis=0, keepdims=True)
            live, scale = factor(2 + i, 2 + j, start, OWN_PART)
            weight_own[pl.ds(index, 1), at] = jnp.where(live, scale * density, 0.0)
        return 0

    lax.fori_loop(0, ROWS // OWN_PART, own_part, 0)

    for e in range(2):
        k_copy(1 - e).wait_recv()
        k_forward(e).start()
    for e in range(2):
        pltpu.make_async_remote_copy(
            src_ref=got_k.at[e, core],
            dst_ref=got_k.at[e, 1 - core],
            send_sem=kf_send.at[e],
            recv_sem=kf_recv.at[e],
            device_id=twin,
            device_id_type=MESH,
        ).wait_recv()
        for j in range(2):
            turned = across(wide_eye, got_k[e, j])
            for i in range(2):
                at = pl.ds(i * NG, NG)
                mix[e, j, at, :] = (sums[6 * i + 4 * e + j] + turned[i * NG:(i + 1) * NG]).astype(BF16)

    acc[...] = jnp.zeros_like(acc)

    def put(e, slot, size, value):
        high = value.astype(BF16)
        zs[e, slot, 0, :, 0:size] = high
        zs[e, slot, 1, :, 0:size] = (value - high.astype(F32)).astype(BF16)

    def gram(e, slot, size, rows):
        return across(rows, zs[e, slot, 0, :, 0:size]) + across(rows, zs[e, slot, 1, :, 0:size])

    def weigh(e, start, size):
        mine_at = pl.ds(there(e, start), size)
        at = pl.ds(start, size)
        y = [own[i, :, mine_at].astype(F32) for i in range(2)]
        weights = []
        for j in range(2):
            left = jnp.dot(mix[e, j], got[e, j, :, at], preferred_element_type=F32)
            each = []
            for i in range(2):
                density = jnp.sum(left[i * NG:(i + 1) * NG] * y[i], axis=0, keepdims=True)
                live, scale = factor(2 + i, 4 * e + j, there(e, start), size)
                each.append(jnp.where(live, scale * density, 0.0))
            weights.append(each)
        return weights

    def from_own(start, size):
        at = pl.ds(start, size)
        y = [own[i, :, at].astype(F32) for i in range(2)]
        mine = [weight_own[pl.ds(index, 1), at] for index in range(3)]
        return (2.0 * mine[0] * y[0] + mine[1] * y[1], mine[1] * y[0] + 2.0 * mine[2] * y[1])

    def from_got(e, start, size, weights):
        x = [got[e, j, :, pl.ds(start, size)].astype(F32) for j in range(2)]
        return tuple(weights[0][i] * x[0] + weights[1][i] * x[1] for i in range(2))

    def one_way(e, start, size):
        weights = weigh(e, start, size)
        y = [own[i, :, pl.ds(there(e, start), size)].astype(F32) for i in range(2)]
        for j in range(2):
            put(e, 2 + j, size, weights[j][0] * y[0] + weights[j][1] * y[1])
        a = from_got(e, start, size, weights)
        b = from_own(there(e, start), size)
        for i in range(2):
            put(e, i, size, a[i] + b[i])

    def both_ways(start, size):
        a = from_got(0, start, size, weigh(0, start, size))
        b = from_got(1, start, size, weigh(1, start, size))
        c = from_own(start, size)
        for i in range(2):
            put(0, i, size, a[i] + b[i] + c[i])

    def add_theirs(e, start, size):
        for j in range(2):
            acc[2 + 2 * e + j] += gram(e, 2 + j, size, got[e, j, :, pl.ds(start, size)])

    def add_mine(e, start, size):
        for i in range(2):
            acc[i] += gram(e, i, size, own[i, :, pl.ds(there(e, start), size)])

    keep = pl.ds(pl.multiple_of(core * OUT, 32), OUT)
    give = pl.ds(pl.multiple_of((1 - core) * OUT, 32), OUT)
    swaps = [
        pltpu.make_async_remote_copy(
            src_ref=acc.at[pl.ds(start, 2), give],
            dst_ref=got_pair.at[pl.ds(start, 2)],
            send_sem=pair_send.at[n],
            recv_sem=pair_recv.at[n],
            device_id=twin,
            device_id_type=MESH,
        )
        for n, start in enumerate((2, 4, 0))
    ]

    def step(k, _):
        for e in range(2):
            row_copy(e, k).wait_send()

            @pl.when(k + 2 < PARTS)
            def _():
                row_copy(e, k + 2).start()

            for later in (PARTS, PARTS + 1):
                @pl.when(k + 2 == later)
                def _():
                    row_copy(e, later).start()

        for e in range(2):
            row_copy(1 - e, k).wait_recv()
            start = pl.multiple_of(k * PART, 128)
            one_way(e, start, PART)
            add_theirs(e, start, PART)
            add_mine(e, start, PART)
        return 0

    lax.fori_loop(0, PARTS, step, 0)

    for k in range(PARTS, COPIES - 1):
        for e in range(2):
            row_copy(e, k).wait_send()
            if k + 2 < COPIES:
                row_copy(e, k + 2).start()
        for e in range(2):
            row_copy(1 - e, k).wait_recv()
            one_way(e, STARTS[k], SIZES[k])
            add_theirs(e, STARTS[k], SIZES[k])
            if k == COPIES - 2:
                swaps[e].start()
            else:
                add_mine(e, STARTS[k], SIZES[k])
    for e in range(2):
        add_mine(e, STARTS[-2], SIZES[-2])

    results = [
        pltpu.make_async_remote_copy(
            src_ref=send_res.at[e],
            dst_ref=got_res.at[1 - e],
            send_sem=res_send.at[e],
            recv_sem=res_recv.at[1 - e],
            device_id=sides[e],
            device_id_type=MESH,
        )
        for e in range(2)
    ]
    norm = AUXB ** (-0.5)
    for e in range(2):
        swaps[e].wait_recv()
        both = [acc[2 + 2 * e + j, keep, :] + got_pair[2 + 2 * e + j] for j in range(2)]
        send_res[e] = jnp.concatenate([(total * norm).astype(BF16) for total in both], axis=1)
        results[e].start()
    for e in range(2):
        row_copy(e, COPIES - 1).wait_send()
        row_copy(1 - e, COPIES - 1).wait_recv()
    both_ways(STARTS[-1], BOTH)
    add_mine(0, STARTS[-1], BOTH)
    swaps[2].start()
    swaps[2].wait_recv()
    for i in range(2):
        out[i] = (acc[i, keep, :] + got_pair[i]) * norm
    for e in range(2):
        results[1 - e].wait_recv()
        for i in range(2):
            out[i] += got_res[e, :, i * NG:(i + 1) * NG].astype(F32)
    for e in range(2):
        k_copy(e).wait_send()
        k_forward(e).wait_send()
        results[e].wait_send()
    for swap in swaps:
        swap.wait_send()


def shards(coeffs, kernel, metric, counts, pairs):
    anywhere = pl.BlockSpec(memory_space=pl.ANY)
    scalars = pl.BlockSpec(memory_space=pltpu.SMEM)
    dma = pltpu.SemaphoreType.DMA
    return pl.pallas_call(
        body,
        out_shape=jax.ShapeDtypeStruct((2, OUT, NG), F32),
        in_specs=[anywhere, anywhere, anywhere, scalars, scalars],
        out_specs=pl.BlockSpec(memory_space=pltpu.VMEM),
        scratch_shapes=[
            pltpu.VMEM((2, NG, ROWS), BF16),
            pltpu.VMEM((2, 2, NG, ONE + BOTH), BF16),
            pltpu.VMEM((PAIRS, NG, NG), BF16),
            pltpu.VMEM((NBLK, ROWS), F32),
            pltpu.VMEM((8, ROWS), F32),
            pltpu.VMEM((12, NG, NG), F32),
            pltpu.VMEM((2, NG, 2 * NG), BF16),
            pltpu.VMEM((2, 2, NG, 2 * NG), BF16),
            pltpu.VMEM((2, 2, 2 * NG, NG), BF16),
            pltpu.VMEM((3, NG, NG), BF16),
            pltpu.VMEM((8, ROWS), F32),
            pltpu.VMEM((2, 4, 2, NG, PART), BF16),
            pltpu.VMEM((6, NG, NG), F32),
            pltpu.VMEM((6, OUT, NG), F32),
            pltpu.VMEM((2, OUT, 2 * NG), BF16),
            pltpu.VMEM((2, OUT, 2 * NG), BF16),
            dma((3,)),
            dma((2, COPIES)),
            dma((2, COPIES)),
            dma((2,)),
            dma((2,)),
            dma((2,)),
            dma((2,)),
            dma((3,)),
            dma((3,)),
            dma((2,)),
            dma((2,)),
        ],
        compiler_params=pltpu.CompilerParams(
            collective_id=0, has_side_effects=True, vmem_limit_bytes=58 * 2 ** 20
        ),
        cost_estimate=pl.CostEstimate(
            flops=30 * 10 ** 9, bytes_accessed=14 * 10 ** 6, transcendentals=0
        ),
    )(jnp.transpose(coeffs, (0, 2, 1)), kernel, metric, counts, jnp.transpose(pairs))


def solution(mesh):
    in_specs = (
        P("curve", "aux", None),
        P("curve", None, None),
        P(None, "aux"),
        P(),
        P("curve", None),
    )
    out_specs = P("curve", "aux", None)
    return jax.shard_map(shards, mesh=mesh, in_specs=in_specs, out_specs=out_specs, check_vma=False)
```

time: 139 us -> 124 us (0.89)
  Pallas kernels: 136 us -> 122 us
    pallas_call x1, Pallas kernels: 136 us -> 122 us  [shards(): pl.pallas_call(body, out_shape=jax.ShapeDtypeStruct((2, OUT, NG), F32), i...]
    unnamed x2 -> x1, local copies, waits for them, and re-layouts: 3.19 us -> 1.84 us
where the time goes in v2:
time: 124 us
  Pallas kernels  122 us (98%)
  local copies, waits for them, and re-layouts  1.84 us (1%)
    pallas_call x1, Pallas kernels, shards(): pl.pallas_call(body, out_shape=jax.ShapeDtypeStruct((2, OUT, NG), F32), i...  122 us

profile of v2, /device:TPU:1, one launch (start us, length us, event | category | flops | bytes accessed | tf_op | source)
XLA Modules:
  0.0 123.6 jit_solution(7493723823364359445)
XLA Ops:
  0.0 121.8 %shard_map.55 = f32[2,160,320]{2,1,0:T(8,128)} custom-call(bf16[2,320,6400]{2,1,0:T(8,128)(2,1)} %bitcast.2, bf16[8,320,320]{2,1,0:T(8,128)(2,1)} %kernel.1, f32[128,6400]{1,0:T(8,128)} %metric.1, s32[128]{0:T(128)} %counts.1, s32[2,8]{1,0:T(2,128)} %bitcast.3), custom_call_target="tpu_custom_call" | custom-call | flops 30000001024 | bytes 14000000 | tf_op jit(solution)/shard_map/pallas_call | solution.py:342
  121.8 1.8 %copy.7 = f32[2,160,320]{2,1,0:T(8,128)} copy(f32[2,160,320]{2,1,0:T(8,128)} %shard_map.55) | data formatting | bytes 819200

commit v3 on v2

--- a/solution.py
+++ b/solution.py
@@ -45,10 +45,18 @@
     before = lax.rem(here + RING - 1, RING)
     sides = ((before, core), (after, core))
     twin = (here, 1 - core)
+    there_is = (here > 0, here < RING - 1)
+
+    def for_side(e):
+        return pl.when(there_is[e])
+
 
     barrier = pltpu.get_barrier_semaphore()
-    for target in (*sides, twin):
-        pl.semaphore_signal(barrier, inc=1, device_id=target, device_id_type=MESH)
+    pl.semaphore_signal(barrier, inc=1, device_id=twin, device_id_type=MESH)
+    for e in range(2):
+        @for_side(e)
+        def _():
+            pl.semaphore_signal(barrier, inc=1, device_id=sides[e], device_id_type=MESH)
 
     loads = [
         pltpu.make_async_copy(kernel, blocks, load_sem.at[0]),
@@ -57,7 +65,15 @@
     ]
     for load in loads:
         load.start()
-    pl.semaphore_wait(barrier, 3)
+
+    for e in range(2):
+        @pl.when(jnp.logical_not(there_is[e]))
+        def _():
+            got[e] = jnp.zeros_like(got[e])
+            got_k[e] = jnp.zeros_like(got_k[e])
+            got_res[e] = jnp.zeros_like(got_res[e])
+
+    pl.semaphore_wait(barrier, 1 + there_is[0].astype(jnp.int32) + there_is[1].astype(jnp.int32))
 
     def k_copy(e):
         return pltpu.make_async_remote_copy(
@@ -98,8 +114,23 @@
             device_id_type=MESH,
         )
 
-    for e in range(2):
-        row_copy(e, 0).start()
+    def send_rows(e, k):
+        @for_side(e)
+        def _():
+            row_copy(e, k).start()
+
+    def rows_sent(e, k):
+        @for_side(e)
+        def _():
+            row_copy(e, k).wait_send()
+
+    def rows_here(e, k):
+        @for_side(e)
+        def _():
+            row_copy(1 - e, k).wait_recv()
+
+    for e in range(2):
+        send_rows(e, 0)
     loads[0].wait()
 
     first = [pairs[0, p] - 2 * here for p in range(PAIRS)]
@@ -126,9 +157,13 @@
     for e in range(2):
         both = [sums[6 * core + 4 * e + j].astype(BF16) for j in range(2)]
         sent_k[e] = jnp.concatenate(both, axis=1)
-        k_copy(e).start()
-    for e in range(2):
-        row_copy(e, 1).start()
+
+        @for_side(e)
+        def _():
+            k_copy(e).start()
+
+    for e in range(2):
+        send_rows(e, 1)
 
     wide_eye = (
         lax.broadcasted_iota(jnp.int32, (2 * NG, 2 * NG), 0)
@@ -167,17 +202,23 @@
     lax.fori_loop(0, ROWS // OWN_PART, own_part, 0)
 
     for e in range(2):
-        k_copy(1 - e).wait_recv()
-        k_forward(e).start()
-    for e in range(2):
-        pltpu.make_async_remote_copy(
-            src_ref=got_k.at[e, core],
-            dst_ref=got_k.at[e, 1 - core],
-            send_sem=kf_send.at[e],
-            recv_sem=kf_recv.at[e],
-            device_id=twin,
-            device_id_type=MESH,
-        ).wait_recv()
+        @for_side(e)
+        def _():
+            k_copy(1 - e).wait_recv()
+            k_forward(e).start()
+
+    for e in range(2):
+        @for_side(e)
+        def _():
+            pltpu.make_async_remote_copy(
+                src_ref=got_k.at[e, core],
+                dst_ref=got_k.at[e, 1 - core],
+                send_sem=kf_send.at[e],
+                recv_sem=kf_recv.at[e],
+                device_id=twin,
+                device_id_type=MESH,
+            ).wait_recv()
+
         for j in range(2):
             turned = across(wide_eye, got_k[e, j])
             for i in range(2):
@@ -260,19 +301,19 @@
 
     def step(k, _):
         for e in range(2):
-            row_copy(e, k).wait_send()
+            rows_sent(e, k)
 
             @pl.when(k + 2 < PARTS)
             def _():
-                row_copy(e, k + 2).start()
+                send_rows(e, k + 2)
 
             for later in (PARTS, PARTS + 1):
                 @pl.when(k + 2 == later)
                 def _():
-                    row_copy(e, later).start()
+                    send_rows(e, later)
 
         for e in range(2):
-            row_copy(1 - e, k).wait_recv()
+            rows_here(e, k)
             start = pl.multiple_of(k * PART, 128)
             one_way(e, start, PART)
             add_theirs(e, start, PART)
@@ -283,11 +324,11 @@
 
     for k in range(PARTS, COPIES - 1):
         for e in range(2):
-            row_copy(e, k).wait_send()
+            rows_sent(e, k)
             if k + 2 < COPIES:
-                row_copy(e, k + 2).start()
+                send_rows(e, k + 2)
         for e in range(2):
-            row_copy(1 - e, k).wait_recv()
+            rows_here(e, k)
             one_way(e, STARTS[k], SIZES[k])
             add_theirs(e, STARTS[k], SIZES[k])
             if k == COPIES - 2:
@@ -313,10 +354,14 @@
         swaps[e].wait_recv()
         both = [acc[2 + 2 * e + j, keep, :] + got_pair[2 + 2 * e + j] for j in range(2)]
         send_res[e] = jnp.concatenate([(total * norm).astype(BF16) for total in both], axis=1)
-        results[e].start()
-    for e in range(2):
-        row_copy(e, COPIES - 1).wait_send()
-        row_copy(1 - e, COPIES - 1).wait_recv()
+
+        @for_side(e)
+        def _():
+            results[e].start()
+
+    for e in range(2):
+        rows_sent(e, COPIES - 1)
+        rows_here(e, COPIES - 1)
     both_ways(STARTS[-1], BOTH)
     add_mine(0, STARTS[-1], BOTH)
     swaps[2].start()
@@ -324,13 +369,19 @@
     for i in range(2):
         out[i] = (acc[i, keep, :] + got_pair[i]) * norm
     for e in range(2):
-        results[1 - e].wait_recv()
+        @for_side(e)
+        def _():
+            results[1 - e].wait_recv()
+
         for i in range(2):
             out[i] += got_res[e, :, i * NG:(i + 1) * NG].astype(F32)
     for e in range(2):
-        k_copy(e).wait_send()
-        k_forward(e).wait_send()
-        results[e].wait_send()
+        @for_side(e)
+        def _():
+            k_copy(e).wait_send()
+            k_forward(e).wait_send()
+            results[e].wait_send()
+
     for swap in swaps:
         swap.wait_send()
 

time: 124 us -> 118 us (0.952)
  the two profiles are of different devices: /device:TPU:1 before, /device:TPU:97 now
where the time goes in v3:
time: 118 us
  Pallas kernels  116 us (98%)
  local copies, waits for them, and re-layouts  1.84 us (2%)
    pallas_call x1, Pallas kernels, shards(): pl.pallas_call(body, out_shape=jax.ShapeDtypeStruct((2, OUT, NG), F32), i...  116 us

profile of v3, /device:TPU:97, one launch (start us, length us, event | category | flops | bytes accessed | tf_op | source)
XLA Modules:
  0.0 118.0 jit_solution(8648446584201639106)
XLA Ops:
  0.0 116.1 %shard_map.55 = f32[2,160,320]{2,1,0:T(8,128)} custom-call(bf16[2,320,6400]{2,1,0:T(8,128)(2,1)} %bitcast.2, bf16[8,320,320]{2,1,0:T(8,128)(2,1)} %kernel.1, f32[128,6400]{1,0:T(8,128)} %metric.1, s32[128]{0:T(128)} %counts.1, s32[2,8]{1,0:T(2,128)} %bitcast.3), custom_call_target="tpu_custom_call" | custom-call | flops 30000001024 | bytes 14000000 | tf_op jit(solution)/shard_map/pallas_call | solution.py:393
  116.1 1.8 %copy.7 = f32[2,160,320]{2,1,0:T(8,128)} copy(f32[2,160,320]{2,1,0:T(8,128)} %shard_map.55) | data formatting | bytes 819200

commit v4 on v3

--- a/solution.py
+++ b/solution.py
@@ -335,8 +335,6 @@
                 swaps[e].start()
             else:
                 add_mine(e, STARTS[k], SIZES[k])
-    for e in range(2):
-        add_mine(e, STARTS[-2], SIZES[-2])
 
     results = [
         pltpu.make_async_remote_copy(
@@ -360,6 +358,8 @@
             results[e].start()
 
     for e in range(2):
+        add_mine(e, STARTS[-2], SIZES[-2])
+    for e in range(2):
         rows_sent(e, COPIES - 1)
         rows_here(e, COPIES - 1)
     both_ways(STARTS[-1], BOTH)
@@ -392,7 +392,7 @@
     dma = pltpu.SemaphoreType.DMA
     return pl.pallas_call(
         body,
-        out_shape=jax.ShapeDtypeStruct((2, OUT, NG), F32),
+        out_shape=pltpu.VMEM((2, OUT, NG), F32),
         in_specs=[anywhere, anywhere, anywhere, scalars, scalars],
         out_specs=pl.BlockSpec(memory_space=pltpu.VMEM),
         scratch_shapes=[

time: 118 us -> 116 us (0.983)
    pallas_call x1, Pallas kernels: 116 us -> 115 us  [shards(): pl.pallas_call(body, out_shape=pltpu.VMEM((2, OUT, NG), F32), in_specs=[a...]
where the time goes in v4:
time: 116 us; the launch traced here: 115 us
  Pallas kernels  115 us (99%)
    pallas_call x1, Pallas kernels, shards(): pl.pallas_call(body, out_shape=pltpu.VMEM((2, OUT, NG), F32), in_specs=[a...  115 us

profile of v4, /device:TPU:97, one launch (start us, length us, event | category | flops | bytes accessed | tf_op | source)
XLA Modules:
  0.0 115.5 jit_solution(3118400341691838455)
XLA Ops:
  0.0 114.7 %shard_map.55 = f32[2,160,320]{2,1,0:T(8,128)S(1)} custom-call(bf16[2,320,6400]{2,1,0:T(8,128)(2,1)} %bitcast.2, bf16[8,320,320]{2,1,0:T(8,128)(2,1)} %kernel.1, f32[128,6400]{1,0:T(8,128)} %metric.1, s32[128]{0:T(128)} %counts.1, s32[2,8]{1,0:T(2,128)} %bitcast.3), custom_call_target="tpu_custom_call" | custom-call | flops 30000001024 | bytes 14000000 | tf_op jit(solution)/shard_map/pallas_call | solution.py:393
  114.7 0.8 copy.7

commit v5 on v4

--- a/solution.py
+++ b/solution.py
@@ -33,7 +33,8 @@
 
 
 def body(
-    coeffs, kernel, metric, counts, pairs, out,
+    coeffs, kernel, metric, counts_in, pairs_in, out,
+    counts, pairs,
     own, got, blocks, met, near, sums, sent_k, got_k, mix, mix_own, weight_own, zs, acc,
     got_pair, send_res, got_res,
     load_sem, row_send, row_recv, k_send, k_recv, kf_send, kf_recv,
@@ -57,14 +58,6 @@
         @for_side(e)
         def _():
             pl.semaphore_signal(barrier, inc=1, device_id=sides[e], device_id_type=MESH)
-
-    loads = [
-        pltpu.make_async_copy(kernel, blocks, load_sem.at[0]),
-        pltpu.make_async_copy(metric, met, load_sem.at[1]),
-        pltpu.make_async_copy(coeffs, own, load_sem.at[2]),
-    ]
-    for load in loads:
-        load.start()
 
     for e in range(2):
         @pl.when(jnp.logical_not(there_is[e]))
@@ -131,7 +124,17 @@
 
     for e in range(2):
         send_rows(e, 0)
+    loads = [
+        pltpu.make_async_copy(kernel, blocks, load_sem.at[0]),
+        pltpu.make_async_copy(metric, met, load_sem.at[1]),
+        pltpu.make_async_copy(coeffs, own, load_sem.at[2]),
+        pltpu.make_async_copy(pairs_in, pairs, load_sem.at[3]),
+        pltpu.make_async_copy(counts_in, counts, load_sem.at[4]),
+    ]
+    for load in loads:
+        load.start()
     loads[0].wait()
+    loads[3].wait()
 
     first = [pairs[0, p] - 2 * here for p in range(PAIRS)]
     second = [pairs[1, p] - 2 * here + 2 for p in range(PAIRS)]
@@ -171,6 +174,7 @@
     ).astype(BF16)
     eye = wide_eye[:NG, :NG]
     loads[1].wait()
+    loads[4].wait()
     loads[2].wait()
     mix_own[0] = sums[2].astype(BF16)
     mix_own[2] = sums[9].astype(BF16)
@@ -388,14 +392,15 @@
 
 def shards(coeffs, kernel, metric, counts, pairs):
     anywhere = pl.BlockSpec(memory_space=pl.ANY)
-    scalars = pl.BlockSpec(memory_space=pltpu.SMEM)
     dma = pltpu.SemaphoreType.DMA
     return pl.pallas_call(
         body,
         out_shape=pltpu.VMEM((2, OUT, NG), F32),
-        in_specs=[anywhere, anywhere, anywhere, scalars, scalars],
+        in_specs=[anywhere] * 5,
         out_specs=pl.BlockSpec(memory_space=pltpu.VMEM),
         scratch_shapes=[
+            pltpu.SMEM((NBLK,), jnp.int32),
+            pltpu.SMEM((2, PAIRS), jnp.int32),
             pltpu.VMEM((2, NG, ROWS), BF16),
             pltpu.VMEM((2, 2, NG, ONE + BOTH), BF16),
             pltpu.VMEM((PAIRS, NG, NG), BF16),
@@ -412,7 +417,7 @@
             pltpu.VMEM((6, OUT, NG), F32),
             pltpu.VMEM((2, OUT, 2 * NG), BF16),
             pltpu.VMEM((2, OUT, 2 * NG), BF16),
-            dma((3,)),
+            dma((5,)),
             dma((2, COPIES)),
             dma((2, COPIES)),
             dma((2,)),

time: 116 us -> 115 us (level)
  no operation moved by 1% of the time
where the time goes in v5:
time: 115 us
  Pallas kernels  114 us (99%)
    pallas_call x1, Pallas kernels, shards(): pl.pallas_call(body, out_shape=pltpu.VMEM((2, OUT, NG), F32), in_specs=[a...  114 us

profile of v5, /device:TPU:97, one launch (start us, length us, event | category | flops | bytes accessed | tf_op | source)
XLA Modules:
  0.0 114.8 jit_solution(1034729171277661270)
XLA Ops:
  0.0 114.0 %shard_map.55 = f32[2,160,320]{2,1,0:T(8,128)S(1)} custom-call(bf16[2,320,6400]{2,1,0:T(8,128)(2,1)} %bitcast.2, bf16[8,320,320]{2,1,0:T(8,128)(2,1)} %kernel.1, f32[128,6400]{1,0:T(8,128)} %metric.1, s32[128]{0:T(128)} %counts_in.1, s32[2,8]{1,0:T(2,128)} %bitcast.3), custom_call_target="tpu_custom_call" | custom-call | flops 30000001024 | bytes 14000000 | tf_op jit(solution)/shard_map/pallas_call | solution.py:396
  114.0 0.8 copy.7
